TPU v7x, 128 devices: a whole 4x4x4 slice. The times are simulated.
128 devices in a mesh: tm: 8 (over y, core), expert: 16 (over z, x).
Axes of the slice: x: 4, y: 4, z: 4, core: 2. Of those that a mesh axis runs over, the one named last changes fastest.
Arguments:
- queries: bfloat16 [16384, 2048], P(('tm', 'expert')), may hold values from -6 to 6
- keys: bfloat16 [16384, 2048], P(('tm', 'expert')), may hold values from -6 to 6
- values: bfloat16 [16384, 2048], P(('tm', 'expert')), may hold values from -6 to 6
- out_grad: bfloat16 [16384, 2048], P(('tm', 'expert')), may hold values from -6 to 6
- expert_ids: int32 [16384, 2], P(('tm', 'expert')), may hold values from 0 to 31, all different within a row
- combine_gates: float32 [16384, 2], P(('tm', 'expert')), may hold values from 0.2 to 1
- gate_weight: bfloat16 [128, 2048, 512], P(('tm', 'expert')), may hold values from -0.125 to 0.125
- up_weight: bfloat16 [128, 2048, 512], P(('tm', 'expert')), may hold values from -0.125 to 0.125
- down_weight: bfloat16 [128, 512, 2048], P(('tm', 'expert')), may hold values from -0.125 to 0.125
Outputs:
- query_grad: bfloat16 [16384, 2048], P(('tm', 'expert'))
- key_grad: bfloat16 [16384, 2048], P(('tm', 'expert'))
- value_grad: bfloat16 [16384, 2048], P(('tm', 'expert'))
- gate_weight_grad: float32 [128, 2048, 512], P(('tm', 'expert'))
- up_weight_grad: float32 [128, 2048, 512], P(('tm', 'expert'))
- down_weight_grad: float32 [128, 512, 2048], P(('tm', 'expert'))
Inputs may be any that keep to these rules, and one draw needn't show every extreme that they name: `expert_ids`: the two experts of a token differ.
All inputs are finite; a program needn't handle non-finite values.
Results may differ from a plain program's by a relative error of at most 0.017.
Values may be sent and summed in bfloat16 or wider, within the bound.
A program may use at most 192 MiB of HBM per device.

v0:
```python
import jax
import jax.numpy as jnp
from jax import lax
from jax.sharding import PartitionSpec as P

HEADS = 16
HEAD_DIM = 128
SLICES = 4


epsilon = 1e-06
highest = lax.Precision.HIGHEST


def side_by_side(arrays, axis, split_dim, concat_dim, along):
    widths = [a.shape[along] for a in arrays]
    both = jnp.concatenate(arrays, axis=along)
    whole = lax.all_to_all(both, axis, split_axis=split_dim, concat_axis=concat_dim, tiled=True)
    return tuple(jnp.split(whole, [sum(widths[:k]) for k in range(1, len(widths))], axis=along))


def slot_places(routes, capacity, experts):
    flat_ids = routes.reshape(-1)
    onehot = (flat_ids[:, None] == jnp.arange(experts, dtype=jnp.int32)[None, :]).astype(jnp.int32)
    earlier = jnp.cumsum(onehot, axis=0) - onehot
    position = jnp.sum(earlier * onehot, axis=1)
    return jnp.where(position < capacity, flat_ids * capacity + position, experts * capacity)


def expert_slice(rows, grad_rows, gate_part, up_part, down_part):
    gate = jnp.dot(rows, gate_part, preferred_element_type=jnp.float32)
    upper = jnp.dot(rows, up_part, preferred_element_type=jnp.float32)
    sigma = jax.nn.sigmoid(gate)
    act = (gate * sigma * upper).astype(jnp.bfloat16)
    act_grad = jnp.dot(grad_rows, down_part.T, preferred_element_type=jnp.float32)
    down_grad = jnp.dot(act.T, grad_rows, preferred_element_type=jnp.float32)
    gate_grad = (act_grad * upper * sigma * (1.0 + gate * (1.0 - sigma))).astype(jnp.bfloat16)
    up_grad = (act_grad * gate * sigma).astype(jnp.bfloat16)
    gate_wgrad = jnp.dot(rows.T, gate_grad, preferred_element_type=jnp.float32)
    up_wgrad = jnp.dot(rows.T, up_grad, preferred_element_type=jnp.float32)
    partial_sum = jnp.dot(gate_grad, gate_part.T, preferred_element_type=jnp.float32)
    partial_sum = partial_sum + jnp.dot(up_grad, up_part.T, preferred_element_type=jnp.float32)
    return (partial_sum.astype(jnp.bfloat16), gate_wgrad, up_wgrad, down_grad)


def body(
    queries, keys, values, out_grad, expert_ids, combine_gates, gate_weight, up_weight, down_weight
):
    tok_rows = queries.shape[0]
    width = queries.shape[1]
    time_count = lax.axis_size("tm")
    group_count = lax.axis_size("expert")
    devices = time_count * group_count
    experts = devices // SLICES
    capacity = SLICES * max(1, 3 * tok_rows // (experts * SLICES))
    shape3 = (tok_rows, HEADS, HEAD_DIM)
    query_f = queries.astype(jnp.float32).reshape(shape3)
    key_f = keys.astype(jnp.float32).reshape(shape3)
    value_f = values.astype(jnp.float32).reshape(shape3)
    local = jnp.einsum("tha,thb->hab", key_f, value_f, precision=highest)
    everyone = lax.all_gather(local[None], "tm", axis=0, tiled=True)
    mine = lax.axis_index("tm")
    picks = (jnp.arange(everyone.shape[0], dtype=jnp.int32) <= mine).astype(jnp.float32)
    inclusive = jnp.einsum("c,chab->hab", picks, everyone, precision=highest)
    states = lax.psum(inclusive, "expert")
    mixed = jnp.einsum("tha,hab->thb", query_f, states, precision=highest)
    scale = lax.rsqrt(jnp.mean(mixed * mixed, axis=-1, keepdims=True) + epsilon)
    normed = mixed * scale
    hidden = normed.astype(jnp.bfloat16).reshape(tok_rows, width)
    places = slot_places(expert_ids, capacity, experts)
    rows_h = jnp.repeat(hidden, 2, axis=0)
    grad_f = out_grad.astype(jnp.float32)
    rows_g = (jnp.repeat(grad_f, 2, axis=0) * combine_gates.reshape(-1, 1)).astype(jnp.bfloat16)
    buffer_h = (
        jnp.zeros((experts * capacity, width), jnp.bfloat16).at[places].set(rows_h, mode="drop")
    )
    buffer_g = (
        jnp.zeros((experts * capacity, width), jnp.bfloat16).at[places].set(rows_g, mode="drop")
    )
    send_h = jnp.repeat(buffer_h.reshape(experts, capacity, width), SLICES, axis=0)
    send_g = jnp.repeat(buffer_g.reshape(experts, capacity, width), SLICES, axis=0)
    got_h, got_g = side_by_side((send_h, send_g), ("tm", "expert"), 0, 0, 1)
    got_h = got_h.reshape(1, devices, capacity, width)
    got_g = got_g.reshape(1, devices, capacity, width)
    rows = got_h.reshape(-1, width)
    grad_rows = got_g.reshape(-1, width)
    partial_sum, gate_wgrad, up_wgrad, down_grad = expert_slice(
        rows, grad_rows, gate_weight[0], up_weight[0], down_weight[0]
    )
    payload = partial_sum.astype(jnp.float32).reshape(devices, capacity, width)
    returned = lax.all_to_all(
        payload.astype(jnp.bfloat16), ("tm", "expert"), split_axis=0, concat_axis=0, tiled=True
    ).astype(payload.dtype)
    summed = jnp.sum(returned.reshape(experts, SLICES, capacity, width), axis=1)
    per_choice = jnp.take(
        summed.reshape(experts * capacity, width), places, axis=0, mode="fill", fill_value=0.0
    )
    moe_grad = jnp.sum(per_choice.reshape(tok_rows, 2, width), axis=1)
    hidden_grad = (grad_f + moe_grad).reshape(shape3)
    norm_grad = scale * (
        hidden_grad - normed * jnp.mean(hidden_grad * normed, axis=-1, keepdims=True)
    )
    query_grad = jnp.einsum("thb,hab->tha", norm_grad, states, precision=highest)
    local_back = jnp.einsum("tha,thb->hab", query_f, norm_grad, precision=highest)
    every_back = lax.all_gather(
        local_back[None].astype(jnp.bfloat16), "tm", axis=0, tiled=True
    ).astype(jnp.float32)
    mine_back = lax.axis_index("tm")
    picks_back = (jnp.arange(every_back.shape[0], dtype=jnp.int32) >= mine_back).astype(jnp.float32)
    inclusive_back = jnp.einsum("c,chab->hab", picks_back, every_back, precision=highest)
    back_states = lax.psum(inclusive_back.astype(jnp.bfloat16), "expert").astype(jnp.float32)
    key_grad = jnp.einsum("thb,hab->tha", value_f, back_states, precision=highest)
    value_grad = jnp.einsum("tha,hab->thb", key_f, back_states, precision=highest)
    return (
        query_grad.reshape(tok_rows, width).astype(jnp.bfloat16),
        key_grad.reshape(tok_rows, width).astype(jnp.bfloat16),
        value_grad.reshape(tok_rows, width).astype(jnp.bfloat16),
        gate_wgrad[None],
        up_wgrad[None],
        down_grad[None],
    )


def solution(mesh):
    placed = (
        P(("tm", "expert"), None),
        P(("tm", "expert"), None),
        P(("tm", "expert"), None),
        P(("tm", "expert"), None),
        P(("tm", "expert"), None),
        P(("tm", "expert"), None),
        P(("tm", "expert"), None, None),
        P(("tm", "expert"), None, None),
        P(("tm", "expert"), None, None),
    )
    return jax.shard_map(
        body,
        mesh=mesh,
        in_specs=placed,
        out_specs=(
            P(("tm", "expert"), None),
            P(("tm", "expert"), None),
            P(("tm", "expert"), None),
            P(("tm", "expert"), None, None),
            P(("tm", "expert"), None, None),
            P(("tm", "expert"), None, None),
        ),
        check_vma=False,
    )
```

profile of v0, /device:TPU:1, one launch (start us, length us, event | category | flops | bytes accessed | tf_op | source)
XLA Modules:
  0.0 692.8 jit_solution(2359564202389222377)
XLA Ops:
  7.2 2.7 fusion.23
  10.0 53.7 %all-gather.5.cloned.1.call-done = f32[128,128,128]{2,1,0:T(8,128)} async-done(((f32[16,128,128]{2,1,0:T(8,128)}), f32[128,128,128]{2,1,0:T(8,128)}) %all-gather.5.cloned.1.call-update) | async-done | bytes 8388624 | tf_op jit(solution)/shard_map/all_gather | solution.py:61
  63.7 11.8 %fusion = f32[1,16,128,128]{3,0,2,1:T(1,128)S(1)} fusion(f32[8,16,128,128]{3,2,1,0:T(8,128)} %bitcast.136, s32[]{:T(128)S(6)} %axis_index.19), kind=kOutput, calls=%fused_computation.6 | convolution fusion | flops 25165832 | bytes 9437188 | tf_op jit(solution)/shard_map/c,chab->hab/dot_general | solution.py:64
  75.6 2.1 copy.71
  77.7 0.1 copy.52
  77.8 0.1 eq.29
  78.0 0.1 eq.25
  78.1 0.6 reduce-window.6
  78.7 0.2 slice_reduce_fusion
  79.0 0.1 mul.85
  79.1 0.1 copy.57
  79.2 0.1 mul.87
  79.4 3.4 broadcast_in_dim.52
  82.8 3.6 reshape.151
  86.5 4.5 scatter_custom_fusion.1
  91.1 3.6 reshape.152
  94.7 68.6 %all-reduce.3.cloned.1.call-done = f32[16,128,128]{1,2,0:T(8,128)} async-done(((f32[16,128,128]{1,2,0:T(8,128)}), f32[16,128,128]{1,2,0:T(8,128)}) %all-reduce.3.cloned.1.call-update) | async-done | bytes 1048592 | tf_op jit(solution)/shard_map/psum | solution.py:65
  163.3 2.4 multiply_reduce_fusion.1
  165.7 1.0 copy-done.2
  166.7 0.1 multiply_convert_fusion.6
  166.9 1.0 copy.56
  167.9 1.7 broadcast_in_dim.50
  169.5 1.2 reshape.172
  170.8 4.1 scatter_custom_fusion
  174.9 3.6 reshape.149
  178.5 6.1 broadcast_in_dim.53
  184.5 4.3 broadcast_in_dim.51
  188.8 9.2 %pad_maximum_fusion = bf16[128,24,2048]{2,1,0:T(8,128)(2,1)S(1)} fusion(bf16[128,12,2048]{2,1,0:T(8,128)(2,1)} %bitcast.132, bf16[128,12,2048]{2,1,0:T(8,128)(2,1)} %bitcast.133), kind=kLoop, calls=%fused_computation.4 | loop fusion | flops 25165824 | bytes 25165824 | tf_op jit(solution)/shard_map/concatenate | solution.py:17
  198.0 150.5 %all_to_all.10 = bf16[128,24,2048]{2,1,0:T(8,128)(2,1)S(1)} all-to-all(bf16[128,24,2048]{2,1,0:T(8,128)(2,1)S(1)} %pad_maximum_fusion), channel_id=1, replica_groups=mesh['tm'=8,'expert'=16] {'tm','expert'}, dimensions={0} | all-to-all | bytes 25165824 | tf_op jit(solution)/shard_map/all_to_all | solution.py:18
  348.6 7.1 %fusion.46 = (bf16[128,12,2048]{2,1,0:T(8,128)(2,1)}, bf16[128,12,2048]{2,1,0:T(8,128)(2,1)}) fusion(bf16[128,24,2048]{2,1,0:T(8,128)(2,1)S(1)} %all_to_all.10), kind=kLoop, calls=%fused_computation.84 | loop fusion | bytes 25165824 | tf_op jit(solution)/shard_map/split | solution.py:19
  355.7 10.7 %reshape_reshape.6 = bf16[1536,2048]{1,0:T(8,128)(2,1)} reshape(bf16[128,12,2048]{2,1,0:T(8,128)(2,1)} %get-tuple-element.24) | data formatting | bytes 12582912 | tf_op jit(solution)/shard_map/reshape;reshape | solution.py:86
  366.4 10.7 %reshape_reshape.7 = bf16[1536,2048]{1,0:T(8,128)(2,1)} reshape(bf16[128,12,2048]{2,1,0:T(8,128)(2,1)} %get-tuple-element.25) | data formatting | bytes 12582912 | tf_op jit(solution)/shard_map/reshape;reshape | solution.py:85
  377.1 6.0 fusion.6
  383.1 3.4 fusion.9
  386.6 4.8 multiply_convert_fusion.1
  391.5 6.5 fusion.4
  398.0 8.5 %add_convert_fusion = bf16[1536,2048]{1,0:T(8,128)(2,1)} fusion(f32[1536,2048]{1,0:T(8,128)} %fusion.4, bf16[1536,512]{1,0:T(8,128)(2,1)S(1)} %get-tuple-element.26, bf16[1,2048,512]{2,1,0:T(8,128)(2,1)S(1)} %copy-done.13), kind=kOutput, calls=%fused_computation.5 | convolution fusion | flops 3227516928 | bytes 22544384 | tf_op jit(solution)/shard_map/dot_general | solution.py:42
  406.5 10.6 %convert_element_type.88 = bf16[128,12,2048]{2,1,0:T(8,128)(2,1)} reshape(bf16[1536,2048]{1,0:T(8,128)(2,1)} %add_convert_fusion) | data formatting | bytes 12582912 | tf_op jit(solution)/shard_map/convert_element_type | solution.py:92
  417.2 6.4 all-to-all-start.1
  423.6 0.1 reduce_sum.51
  423.8 99.5 %all-to-all-done.1 = bf16[128,12,2048]{2,1,0:T(8,128)(2,1)} async-done(((bf16[128,12,2048]{2,1,0:T(8,128)(2,1)}), bf16[128,12,2048]{2,1,0:T(8,128)(2,1)}, u32[]{:S(2)}, u32[]{:S(2)}) %all-to-all-start.1) | async-done | bytes 6291488 | tf_op jit(solution)/shard_map/all_to_all | solution.py:91
  523.3 7.8 %convert_reduce_fusion = f32[32,12,2048]{2,1,0:T(8,128)} fusion(bf16[128,12,2048]{2,1,0:T(8,128)(2,1)} %all-to-all-done.1), kind=kLoop, calls=%fused_computation.3 | loop fusion | flops 5505024 | bytes 9437184 | tf_op jit(solution)/shard_map/reduce_sum | solution.py:94
  531.2 3.0 reshape.156
  534.2 2.7 gather_fusion
  536.8 2.5 gather.7
  539.3 4.5 select_reduce_fusion
  544.0 0.3 copy.58
  544.3 0.8 copy-done.3
  545.1 0.2 multiply_reduce_fusion
  545.2 1.8 fusion.14
  547.1 1.0 copy.62
  548.2 8.9 %convolution_bitcast_fusion.1 = f32[1,2048,512]{2,1,0:T(8,128)} fusion(bf16[1536,2048]{1,0:T(8,128)(2,1)} %reshape_reshape.7, bf16[1536,512]{1,0:T(8,128)(2,1)} %copy-done.14), kind=kOutput, calls=%fused_computation.11 | convolution fusion | flops 3221225472 | bytes 12058624 | tf_op jit(solution)/shard_map/dot_general | solution.py:40
  557.0 8.3 %convolution_bitcast_fusion = f32[1,512,2048]{2,1,0:T(8,128)} fusion(bf16[1536,2048]{1,0:T(8,128)(2,1)} %reshape_reshape.6, f32[1536,512]{1,0:T(8,128)S(1)} %copy-done.19, f32[1536,512]{1,0:T(8,128)S(1)} %copy-done.17), kind=kOutput, calls=%fused_computation.10 | convolution fusion | flops 3225944064 | bytes 16777216 | tf_op jit(solution)/shard_map/dot_general | solution.py:36
  565.3 25.7 %all-gather.7.cloned.1.call-done = bf16[128,128,128]{2,1,0:T(8,128)(2,1)} async-done(((bf16[16,128,128]{2,1,0:T(8,128)(2,1)}), bf16[128,128,128]{2,1,0:T(8,128)(2,1)}) %all-gather.7.cloned.1.call-update) | async-done | bytes 4194320 | tf_op jit(solution)/shard_map/all_gather | solution.py:105
  591.1 4.9 fusion.2
  596.0 0.9 convert_element_type.95
  596.9 8.8 %convolution_bitcast_fusion.2 = f32[1,2048,512]{2,1,0:T(8,128)} fusion(bf16[1536,2048]{1,0:T(8,128)(2,1)} %reshape_reshape.7, bf16[1536,512]{1,0:T(8,128)(2,1)} %copy-done.15), kind=kOutput, calls=%fused_computation.12 | convolution fusion | flops 3221225472 | bytes 12058624 | tf_op jit(solution)/shard_map/dot_general | solution.py:39
  605.7 2.0 convolution_convert_fusion.3
  607.7 1.0 copy.66
  608.7 71.8 %all-reduce.5.cloned.1.call-done = bf16[16,128,128]{2,1,0:T(8,128)(2,1)} async-done(((bf16[16,128,128]{2,1,0:T(8,128)(2,1)}), bf16[16,128,128]{2,1,0:T(8,128)(2,1)}) %all-reduce.5.cloned.1.call-update) | async-done | bytes 524304 | tf_op jit(solution)/shard_map/psum | solution.py:111
  680.6 1.5 convolution_convert_fusion.1
  682.1 1.0 copy.67
  683.1 1.7 convolution_convert_fusion
  684.8 1.0 copy.68
  (62 shorter events, 0.7 us)
Async XLA Ops:
  7.2 369.9 %copy-start = (bf16[1,2048,512]{2,1,0:T(8,128)(2,1)S(1)}, bf16[1,2048,512]{2,1,0:T(8,128)(2,1)}, u32[]{:S(2)}) copy-start(bf16[1,2048,512]{2,1,0:T(8,128)(2,1)} %param.15) | copy-start | bytes 6291460
  7.2 56.5 %all-gather.5.cloned.1.call-start = ((), (), s32[]{:S(2)}) async-start(), calls=%async_computation.4 | async-start | bytes 9437184 | tf_op jit(solution)/shard_map/all_gather | solution.py:61
  9.9 153.4 %all-reduce.3.cloned.1.call-start = ((), (), s32[]{:S(2)}) async-start(), calls=%async_computation.2 | async-start | bytes 2097152 | tf_op jit(solution)/shard_map/psum | solution.py:65
  75.6 2.1 copy-start.10
  75.6 3.5 copy-start.11
  86.5 76.7 %copy-start.8 = (bf16[128,2048]{1,0:T(8,128)(2,1)S(1)}, bf16[128,2048]{1,0:T(8,128)(2,1)}, u32[]{:S(2)}) copy-start(bf16[128,2048]{1,0:T(8,128)(2,1)} %param.9) | copy-start | bytes 1572868
  165.7 1.0 copy-start.2
  178.5 6.1 copy-start.4
  377.1 6.0 copy-start.5
  377.1 6.0 copy-start.13
  377.1 9.5 %slice-start = ((s8[6291456]{0:T(1024)(128)(4,1)}), s8[4194304]{0:T(1024)(128)(4,1)S(1)}, s32[]{:S(2)}) async-start(s8[6291456]{0:T(1024)(128)(4,1)} %bitcast.137), calls=%async_computation.6 | async-start | bytes 8388608
  383.1 3.5 copy-start.16
  383.1 3.5 slice-start.1
  383.1 3.5 copy-start.12
  386.6 4.9 copy-start.18
  391.5 6.5 copy-start.15
  391.5 6.5 copy-start.14
  417.2 106.2 %all-to-all-start.1 = ((bf16[128,12,2048]{2,1,0:T(8,128)(2,1)}), bf16[128,12,2048]{2,1,0:T(8,128)(2,1)}, u32[]{:S(2)}, u32[]{:S(2)}) async-start(bf16[128,12,2048]{2,1,0:T(8,128)(2,1)} %convert_element_type.88), calls=%async_computation.1 | async-start | bytes 16777216 | tf_op jit(solution)/shard_map/all_to_all | solution.py:91
  423.6 167.5 %all-gather.7.cloned.1.call-start = ((), (), s32[]{:S(2)}) async-start(), calls=%async_computation.5 | async-start | bytes 4718592 | tf_op jit(solution)/shard_map/all_gather | solution.py:105
  539.3 4.5 copy-start.7
  543.8 1.2 copy-start.3
  548.1 132.5 %all-reduce.5.cloned.1.call-start = ((), (), s32[]{:S(2)}) async-start(), calls=%async_computation.3 | async-start | bytes 1048576 | tf_op jit(solution)/shard_map/psum | solution.py:111
  548.1 8.9 %copy-start.17 = (f32[1536,512]{1,0:T(8,128)S(1)}, f32[1536,512]{1,0:T(8,128)}, u32[]{:S(2)}) copy-start(f32[1536,512]{1,0:T(8,128)} %copy-done.16) | copy-start | bytes 9437188
  548.1 8.9 %copy-start.19 = (f32[1536,512]{1,0:T(8,128)S(1)}, f32[1536,512]{1,0:T(8,128)}, u32[]{:S(2)}) copy-start(f32[1536,512]{1,0:T(8,128)} %copy-done.18) | copy-start | bytes 9437188
  596.9 8.8 %copy-start.6 = (f32[16,128,128]{1,2,0:T(8,128)S(1)}, f32[16,128,128]{1,2,0:T(8,128)}, u32[]{:S(2)}) copy-start(f32[16,128,128]{1,2,0:T(8,128)} %all-reduce.3.cloned.1.call-done) | copy-start | bytes 3145732
  605.7 74.9 %copy-start.9 = (bf16[128,2048]{1,0:T(8,128)(2,1)S(1)}, bf16[128,2048]{1,0:T(8,128)(2,1)}, u32[]{:S(2)}) copy-start(bf16[128,2048]{1,0:T(8,128)(2,1)} %param.11) | copy-start | bytes 1572868
  607.7 78.1 %copy-start.1 = (bf16[1,2048,512]{2,1,0:T(8,128)(2,1)S(1)}, bf16[1,2048,512]{2,1,0:T(8,128)(2,1)}, u32[]{:S(2)}) copy-start(bf16[1,2048,512]{2,1,0:T(8,128)(2,1)} %param.15) | copy-start | bytes 6291460
Sparse Core Ops, SparseCore 0:
  10.3 53.3 all-gather.4
  77.8 85.4 all-reduce.2
  548.2 42.8 all-gather.6
  597.1 83.4 all-reduce.4
where the time goes:
time: 702 us; the launch traced here: 693 us
  waiting for transfers between devices  319 us (45%)
  blocking collectives  151 us (22%)
  local copies, waits for them, and re-layouts  89.3 us (13%)
  matrix products  84.1 us (12%)
  other arithmetic  28.2 us (4%)
  between operations  14.6 us (2%)
    all_to_all x1, blocking collectives, side_by_side(): lax.all_to_all(both, axis, split_axis=split_dim, concat_axis=concat_dim,...  151 us
    all_to_all x1, waiting for transfers between devices, body(): lax.all_to_all(payload.astype(jnp.bfloat16), ('tm', 'expert'), split_axis...  99.5 us
    psum x1, waiting for transfers between devices, body(): lax.psum(inclusive_back.astype(jnp.bfloat16), 'expert').astype(jnp.float32)  71.8 us
    psum x1, waiting for transfers between devices, body(): states = lax.psum(inclusive, 'expert')  68.6 us
    all_gather x1, waiting for transfers between devices, body(): everyone = lax.all_gather(local[None], 'tm', axis=0, tiled=True)  53.7 us
    all_gather x1, waiting for transfers between devices, body(): lax.all_gather(local_back[None].astype(jnp.bfloat16), 'tm', axis=0, tiled...  25.7 us
  transfers between devices with their start and end apart: 5, of which 5 were waited for; matrix products, arithmetic and copies ran while one was open for 7% of the time, Pallas kernels for 0%

commit v1 on v0

v1 whole, which is shorter than its diff:
```python
import functools

import jax
import jax.numpy as jnp
from jax import lax
from jax.experimental import pallas as pl
from jax.experimental.pallas import tpu as pltpu
from jax.sharding import PartitionSpec as P

MESH = pl.DeviceIdType.MESH
EPS = 1e-06
TOK = 128
HD = 128
CAP = 12
G = 4 * CAP
NE = 32
ROWS = NE * G
CH = 8 * G
BC = 512
D = 2048
HID = 512
DY = (0, 1, 3, 2)
BF = jnp.bfloat16
F32 = jnp.float32


def nn(a, b):
    return lax.dot_general(a, b, (((1,), (0,)), ((), ())), preferred_element_type=F32)


def nt(a, b):
    return lax.dot_general(a, b, (((1,), (1,)), ((), ())), preferred_element_type=F32)


def tn(a, b):
    return lax.dot_general(a, b, (((0,), (0,)), ((), ())), preferred_element_type=F32)


def mod(a, n):
    return lax.rem(a, jnp.int32(n))


def drain(ref, sem):
    pltpu.make_async_copy(ref, ref, sem).wait()


def remote(src, dst, ssem, rsem, dev):
    pltpu.make_async_remote_copy(
        src_ref=src, dst_ref=dst, send_sem=ssem, recv_sem=rsem, device_id=dev, device_id_type=MESH
    ).start()


def kernel(
    ids, gates, q, k, v, og, wg_h, wu_h, wd_h,
    qg_o, kg_o, vg_o, dwg_o, dwu_o, dwd_o,
    wg, wu, wd, sterm, srecv, sspan, stb, rtm, rt, xq, xg, pm, gs, sg, sh, yb, xb, mx, hid,
    act, gg, ug, part, rin, rout, rcin, rsin, red, rr, mg, stage,
    bterm, bz, bspan, bown, ball, qgs, qgb,
    wsem, st_s, st_r, sp_s, sp_r, sb_s, sb_r, xt_s, xt_r,
    sl_s, sl_r, mc_s, mc_l, mc_r, mc_f, rd_s, ri_r, rc_r, rs_r, rt_s, rt_r, stsem,
    bz_s, bz_r, bp_s, bp_r, bb_s, bb_r, qg_s, qg_r,
):
    tm = lax.axis_index("tm")
    e = lax.axis_index("expert")
    z = lax.div(e, jnp.int32(4))
    x = mod(e, 4)
    y = lax.div(tm, jnp.int32(2))
    c = mod(tm, 2)
    me = tm * 4 + z
    xr = mod(x + 1, 4)
    xl = mod(x + 3, 4)
    xf = mod(x + 2, 4)
    right = (tm, z * 4 + xr)
    left = (tm, z * 4 + xl)

    def cols(b):
        return pl.ds(pl.multiple_of(b * BC, BC), BC)

    bar = pltpu.get_barrier_semaphore()

    def greet_span(i, _):
        pl.semaphore_signal(bar, inc=1, device_id=(tm, mod(e + i, 16)), device_id_type=MESH)
        return 0

    lax.fori_loop(1, 16, greet_span, 0)

    def greet_plane(i, _):
        t = mod(tm + lax.div(i, jnp.int32(4)), 8)
        zz = mod(z + mod(i, 4), 4)
        pl.semaphore_signal(bar, inc=1, device_id=(t, zz * 4 + x), device_id_type=MESH)
        return 0

    lax.fori_loop(4, 32, greet_plane, 0)

    w_copies = []
    for i, (src, dst) in enumerate(((wg_h, wg), (wu_h, wu), (wd_h, wd))):
        cp = pltpu.make_async_copy(src.at[0], dst, wsem.at[i])
        cp.start()
        w_copies.append(cp)

    for h in range(16):
        sl = slice(h * HD, (h + 1) * HD)
        sterm[h] = tn(k[:, sl], v[:, sl]).astype(BF)

    eye = lax.broadcasted_iota(jnp.int32, (TOK, TOK), 0) == lax.broadcasted_iota(
        jnp.int32, (TOK, TOK), 1
    )
    upper = lax.broadcasted_iota(jnp.int32, (TOK, TOK), 0) < lax.broadcasted_iota(
        jnp.int32, (TOK, TOK), 1
    )
    upper = jnp.where(upper, 1.0, 0.0).astype(BF)
    idf = ids[...].astype(F32)
    gf = gates[...]

    def as_row(a, kk):
        return jnp.sum(jnp.where(eye, a[:, kk : kk + 1], 0.0), axis=0, keepdims=True)

    id_rows = [as_row(idf, kk) for kk in range(2)]
    lanes_e = lax.broadcasted_iota(jnp.int32, (NE, TOK), 0).astype(F32)
    hot = [jnp.where(lanes_e == r, 1.0, 0.0) for r in id_rows]
    earlier = nn((hot[0] + hot[1]).astype(BF), upper)
    rtm[...] = jnp.zeros_like(rtm)
    for kk in range(2):
        pos = jnp.sum(hot[kk] * earlier, axis=0, keepdims=True)
        rtm[kk : kk + 1, :] = jnp.where(pos < CAP, id_rows[kk] * G + pos, -4096.0)
        rtm[2 + kk : 3 + kk, :] = as_row(gf, kk)

    pl.semaphore_wait(bar, 43)

    def send_term(i, _):
        eo = mod(e + i, 16)
        ho = mod(eo, 4) * 4 + lax.div(eo, jnp.int32(4))
        remote(sterm.at[ho], srecv.at[e], st_s, st_r, (tm, eo))
        return 0

    lax.fori_loop(1, 16, send_term, 0)
    for i, (src, dst) in enumerate(((rtm, rt), (og, xg), (q, xq))):
        for d in range(1, 4):
            xo = mod(x + d, 4)
            s = src if i == 0 else src.at[:, cols(xo)]
            remote(s, dst.at[x], xt_s.at[i], xt_r.at[i], (tm, z * 4 + xo))
        s = src if i == 0 else src.at[:, cols(x)]
        pltpu.make_async_copy(s, dst.at[x], xt_r.at[i]).start()

    drain(srecv.at[pl.ds(0, 15)], st_r)
    srecv[e] = sterm[x * 4 + z]
    sspan[tm] = jnp.sum(srecv[...].astype(F32), axis=0)

    def send_span(i, _):
        remote(sspan.at[tm], sspan.at[tm], sp_s, sp_r, (mod(tm + i, 8), e))
        return 0

    lax.fori_loop(1, 8, send_span, 0)

    drain(rt, xt_r.at[0])

    def build(b, _):
        r0 = pl.multiple_of(b * 128, 128)
        ridx = (lax.broadcasted_iota(jnp.int32, (128, TOK), 0) + r0).astype(F32)
        acc = jnp.zeros((128, TOK), F32)
        for s in range(4):
            a = rt[s]
            m0 = ridx == a[0:1] + float(s * CAP)
            m1 = ridx == a[1:2] + float(s * CAP)
            pm[pl.ds(r0, 128), s * TOK : (s + 1) * TOK] = jnp.where(m0 | m1, 1.0, 0.0).astype(BF)
            acc = acc + jnp.where(m0, a[2:3], 0.0) + jnp.where(m1, a[3:4], 0.0)
        gs[pl.ds(r0, 128), :] = jnp.broadcast_to(jnp.sum(acc, axis=1, keepdims=True), (128, TOK))
        return 0

    lax.fori_loop(0, ROWS // 128, build, 0)

    def plane_rows(yy):
        return pl.ds(pl.multiple_of(yy * CH, CH), CH)

    def group_rows(g):
        return pl.ds(pl.multiple_of(g * G, G), G)

    def to_plane(src, dst, dcols, ssem, rsem, yy, self_too):
        def one(i, _):
            cc = mod(c + lax.div(i, jnp.int32(4)), 2)
            zz = mod(z + mod(i, 4), 4)
            t = yy * 2 + cc
            d = dst.at[group_rows(me)] if dcols is None else dst.at[group_rows(me), dcols]
            remote(src.at[group_rows(t * 4 + zz)], d, ssem, rsem, (t, zz * 4 + x))
            return 0

        lax.fori_loop(1 if self_too else 0, 8, one, 0)
        if self_too:
            d = dst.at[group_rows(me)] if dcols is None else dst.at[group_rows(me), dcols]
            pltpu.make_async_copy(src.at[group_rows(me)], d, rsem).start()

    def src_plane(j):
        return mod(y - DY[j] + 4, 4)

    def dst_plane(j):
        return mod(y + DY[j], 4)

    big = (yb, xb)
    small = (sg, sh)

    def wait_own(a, j):
        drain(big[a].at[plane_rows(src_plane(j)), cols(x)], sl_r.at[a, j])

    def cast(a, j):
        ref = big[a].at[plane_rows(src_plane(j)), cols(x)]
        remote(ref, ref, mc_s.at[a], mc_l.at[a, j], right)
        remote(ref, ref, mc_s.at[a], mc_r.at[a, j], left)

    def relay(a, j):
        rows = plane_rows(src_plane(j))
        from_left = big[a].at[rows, cols(xl)]
        from_right = big[a].at[rows, cols(xr)]
        drain(from_left, mc_l.at[a, j])
        if j % 2 == 0:
            remote(from_left, from_left, mc_s.at[a], mc_f.at[a, j], right)
        drain(from_right, mc_r.at[a, j])
        if j % 2 == 1:
            remote(from_right, from_right, mc_s.at[a], mc_f.at[a, j], left)

    def far(a, j):
        drain(big[a].at[plane_rows(src_plane(j)), cols(xf)], mc_f.at[a, j])

    drain(xg, xt_r.at[1])
    for j in range(4):
        rows = plane_rows(dst_plane(j))
        got = nn(pm[rows, :], xg[...].reshape(4 * TOK, BC))
        sg[rows, :] = (got * gs[rows, 0:1]).astype(BF)
        to_plane(sg, yb, cols(x), sl_s.at[0], sl_r.at[0, j], dst_plane(j), j == 0)

    drain(sspan.at[pl.ds(0, 7)], sp_r)
    total = jnp.zeros((HD, HD), F32)
    for t in range(8):
        total = total + jnp.where(t <= tm, sspan[t], 0.0)
    stb[z] = total.astype(BF)
    for d in range(1, 4):
        remote(stb.at[z], stb.at[z], sb_s, sb_r, (tm, mod(z + d, 4) * 4 + x))

    wait_own(0, 0)
    cast(0, 0)

    drain(xq, xt_r.at[2])
    drain(stb.at[pl.ds(0, 3)], sb_r)
    for i in range(4):
        sl = slice(i * HD, (i + 1) * HD)
        m = nn(xq[:, :, sl].reshape(4 * TOK, HD), stb[i])
        mx[:, sl] = m
        scale = lax.rsqrt(jnp.mean(m * m, axis=-1, keepdims=True) + EPS)
        hid[:, sl] = (m * scale).astype(BF)
    for j in range(4):
        rows = plane_rows(dst_plane(j))
        sh[rows, :] = nn(pm[rows, :], hid[...]).astype(BF)
        to_plane(sh, xb, cols(x), sl_s.at[1], sl_r.at[1, j], dst_plane(j), j == 0)

    for j in range(1, 4):
        wait_own(0, j)
        cast(0, j)
    for j in range(4):
        relay(0, j)
        wait_own(1, j)
        cast(1, j)

    for cp in w_copies:
        cp.wait()

    def compute(j):
        far(0, j)
        far(1, j)
        rows = plane_rows(src_plane(j))

        def hidden_cols(n, _):
            hc = pl.ds(pl.multiple_of(n * 256, 256), 256)
            gate = nn(xb[rows, :], wg[:, hc])
            up = nn(xb[rows, :], wu[:, hc])
            act_grad = nt(yb[rows, :], wd[hc, :])
            sigma = jax.nn.sigmoid(gate)
            silu = gate * sigma
            act[rows, hc] = (silu * up).astype(BF)
            gg[rows, hc] = (act_grad * up * sigma * (1.0 + gate * (1.0 - sigma))).astype(BF)
            ug[rows, hc] = (act_grad * silu).astype(BF)
            return 0

        lax.fori_loop(0, HID // 256, hidden_cols, 0)

        def part_cols(n, _):
            pc = cols(n)
            part[rows, pc] = (
                nt(gg[rows, :], wg[pc, :]) + nt(ug[rows, :], wu[pc, :])
            ).astype(BF)
            return 0

        lax.fori_loop(0, D // BC, part_cols, 0)
        if j % 2 == 0:
            remote(part.at[rows, cols(xf)], rin.at[j], rd_s, ri_r.at[j], right)
            remote(part.at[rows, cols(xl)], rsin.at[j], rd_s, rs_r.at[j], left)
        else:
            remote(part.at[rows, cols(xf)], rin.at[j], rd_s, ri_r.at[j], left)
            remote(part.at[rows, cols(xr)], rsin.at[j], rd_s, rs_r.at[j], right)

    def add_on(j):
        rows = plane_rows(src_plane(j))
        drain(rin.at[j], ri_r.at[j])
        near = xr if j % 2 == 0 else xl
        rout[j] = (rin[j].astype(F32) + part[rows, cols(near)].astype(F32)).astype(BF)
        remote(rout.at[j], rcin.at[j], rd_s, rc_r.at[j], right if j % 2 == 0 else left)

    def finish(j):
        yy = src_plane(j)
        rows = plane_rows(yy)
        drain(rsin.at[j], rs_r.at[j])
        drain(rcin.at[j], rc_r.at[j])
        red[rows, :] = (
            rcin[j].astype(F32) + rsin[j].astype(F32) + part[rows, cols(x)].astype(F32)
        ).astype(BF)
        to_plane(red, rr, None, rt_s, rt_r.at[j], yy, j == 0)

    def combine(j):
        rows = plane_rows(dst_plane(j))
        drain(rr.at[rows], rt_r.at[j])
        got = tn(pm[rows, :], rr[rows, :])
        if j == 0:
            mg[...] = got
        else:
            mg[...] += got

    def weights_in(s):
        slot = s % 2
        if s >= 2:
            for w, o in ((0, dwg_o), (1, dwu_o)):
                pltpu.make_async_copy(
                    stage.at[slot, w], o.at[0, (s - 2) * 512 : (s - 1) * 512, :], stsem.at[slot, w]
                ).wait()

        def one(n, _):
            r = pl.ds(pl.multiple_of(n * 256, 256), 256)
            xt = xb[:, pl.ds(pl.multiple_of(s * 512 + n * 256, 256), 256)]
            stage[slot, 0, r, :] = tn(xt, gg[...])
            stage[slot, 1, r, :] = tn(xt, ug[...])
            return 0

        lax.fori_loop(0, 2, one, 0)
        for w, o in ((0, dwg_o), (1, dwu_o)):
            pltpu.make_async_copy(
                stage.at[slot, w], o.at[0, s * 512 : (s + 1) * 512, :], stsem.at[slot, w]
            ).start()

    def weights_out(s):
        slot, w = divmod(s, 2)
        o = (dwg_o, dwu_o)[w]
        pltpu.make_async_copy(
            stage.at[slot, w], o.at[0, (2 + slot) * 512 : (3 + slot) * 512, :], stsem.at[slot, w]
        ).wait()

        def one(n, _):
            r = pl.ds(pl.multiple_of(n * 256, 256), 256)
            stage[slot, w, r, :] = tn(act[:, r], yb[:, s * 512 : (s + 1) * 512])
            return 0

        lax.fori_loop(0, 2, one, 0)
        pltpu.make_async_copy(
            stage.at[slot, w], dwd_o.at[0, :, s * 512 : (s + 1) * 512], stsem.at[slot, w]
        ).start()

    relay(1, 0)
    relay(1, 1)
    compute(0)
    relay(1, 2)
    compute(1)
    add_on(0)
    relay(1, 3)
    compute(2)
    add_on(1)
    compute(3)
    add_on(2)
    finish(0)
    weights_in(0)
    add_on(3)
    finish(1)
    weights_in(1)
    finish(2)
    weights_in(2)
    finish(3)
    weights_in(3)
    combine(0)
    weights_out(0)
    combine(1)
    weights_out(1)
    combine(2)
    weights_out(2)
    weights_out(3)
    combine(3)

    for i in range(4):
        sl = slice(i * HD, (i + 1) * HD)
        m = mx[:, sl]
        scale = lax.rsqrt(jnp.mean(m * m, axis=-1, keepdims=True) + EPS)
        normed = m * scale
        hg = xg[:, :, sl].reshape(4 * TOK, HD).astype(F32) + mg[:, sl]
        ng = scale * (hg - normed * jnp.mean(hg * normed, axis=-1, keepdims=True))
        ngb = ng.astype(BF)
        bterm[i] = tn(xq[:, :, sl].reshape(4 * TOK, HD), ngb).astype(BF)
        qgs[:, :, sl] = nt(ngb, stb[i]).astype(BF).reshape(4, TOK, HD)
    for d in range(1, 4):
        zo = mod(z + d, 4)
        remote(bterm.at[zo], bz.at[z], bz_s, bz_r, (tm, zo * 4 + x))
    for d in range(1, 4):
        xo = mod(x + d, 4)
        remote(qgs.at[xo], qgb.at[x], qg_s, qg_r, (tm, z * 4 + xo))
    drain(bz.at[pl.ds(0, 3)], bz_r)
    bz[z] = bterm[z]
    bspan[tm] = jnp.sum(bz[...].astype(F32), axis=0).astype(BF)

    def send_back_span(i, _):
        remote(bspan.at[tm], bspan.at[tm], bp_s, bp_r, (mod(tm + i, 8), e))
        return 0

    lax.fori_loop(1, 8, send_back_span, 0)
    drain(bspan.at[pl.ds(0, 7)], bp_r)
    total = jnp.zeros((HD, HD), F32)
    for t in range(8):
        total = total + jnp.where(t >= tm, bspan[t].astype(F32), 0.0)
    bown[...] = total.astype(BF)

    def send_back(i, _):
        remote(bown, ball.at[e], bb_s, bb_r, (tm, mod(e + i, 16)))
        return 0

    lax.fori_loop(1, 16, send_back, 0)
    drain(qgb.at[pl.ds(0, 3)], qg_r)
    qgb[x] = qgs[x]
    for b in range(4):
        qg_o[:, b * BC : (b + 1) * BC] = qgb[b]
    drain(ball.at[pl.ds(0, 15)], bb_r)
    ball[e] = bown[...]
    for eo in range(16):
        h = (eo % 4) * 4 + eo // 4
        sl = slice(h * HD, (h + 1) * HD)
        kg_o[:, sl] = nt(v[:, sl], ball[eo]).astype(BF)
        vg_o[:, sl] = nn(k[:, sl], ball[eo]).astype(BF)

    drain(sterm.at[pl.ds(0, 15)], st_s)
    drain(sspan.at[pl.ds(0, 7)], sp_s)
    drain(stb.at[pl.ds(0, 3)], sb_s)
    drain(rt.at[pl.ds(0, 3)], xt_s.at[0])
    drain(xg.at[pl.ds(0, 3)], xt_s.at[1])
    drain(xq.at[pl.ds(0, 3)], xt_s.at[2])
    for a in range(2):
        drain(small[a].at[pl.ds(0, 31 * G)], sl_s.at[a])
        for _ in range(3):
            drain(big[a].at[pl.ds(0, ROWS), pl.ds(0, BC)], mc_s.at[a])
    for _ in range(3):
        drain(red, rd_s)
    drain(red.at[pl.ds(0, 31 * G)], rt_s)
    drain(bz.at[pl.ds(0, 3)], bz_s)
    drain(bspan.at[pl.ds(0, 7)], bp_s)
    drain(ball.at[pl.ds(0, 15)], bb_s)
    drain(qgb.at[pl.ds(0, 3)], qg_s)
    for s in range(4):
        slot, w = divmod(s, 2)
        pltpu.make_async_copy(
            stage.at[slot, w], dwd_o.at[0, :, s * 512 : (s + 1) * 512], stsem.at[slot, w]
        ).wait()


def body(queries, keys, values, out_grad, expert_ids, combine_gates, gate_w, up_w, down_w):
    vm = pl.BlockSpec(memory_space=pltpu.VMEM)
    hbm = pl.BlockSpec(memory_space=pl.ANY)
    dma = pltpu.SemaphoreType.DMA
    scratch = [
        pltpu.VMEM((D, HID), BF),
        pltpu.VMEM((D, HID), BF),
        pltpu.VMEM((HID, D), BF),
        pltpu.VMEM((16, HD, HD), BF),
        pltpu.VMEM((16, HD, HD), BF),
        pltpu.VMEM((8, HD, HD), F32),
        pltpu.VMEM((4, HD, HD), BF),
        pltpu.VMEM((8, TOK), F32),
        pltpu.VMEM((4, 8, TOK), F32),
        pltpu.VMEM((4, TOK, BC), BF),
        pltpu.VMEM((4, TOK, BC), BF),
        pltpu.VMEM((ROWS, 4 * TOK), BF),
        pltpu.VMEM((ROWS, TOK), F32),
        pltpu.VMEM((ROWS, BC), BF),
        pltpu.VMEM((ROWS, BC), BF),
        pltpu.VMEM((ROWS, D), BF),
        pltpu.VMEM((ROWS, D), BF),
        pltpu.VMEM((4 * TOK, BC), F32),
        pltpu.VMEM((4 * TOK, BC), BF),
        pltpu.VMEM((ROWS, HID), BF),
        pltpu.VMEM((ROWS, HID), BF),
        pltpu.VMEM((ROWS, HID), BF),
        pltpu.VMEM((ROWS, D), BF),
        pltpu.VMEM((4, CH, BC), BF),
        pltpu.VMEM((4, CH, BC), BF),
        pltpu.VMEM((4, CH, BC), BF),
        pltpu.VMEM((4, CH, BC), BF),
        pltpu.VMEM((ROWS, BC), BF),
        pltpu.VMEM((ROWS, BC), BF),
        pltpu.VMEM((4 * TOK, BC), F32),
        pltpu.VMEM((2, 2, 512, 512), F32),
        pltpu.VMEM((4, HD, HD), BF),
        pltpu.VMEM((4, HD, HD), BF),
        pltpu.VMEM((8, HD, HD), BF),
        pltpu.VMEM((HD, HD), BF),
        pltpu.VMEM((16, HD, HD), BF),
        pltpu.VMEM((4, TOK, BC), BF),
        pltpu.VMEM((4, TOK, BC), BF),
        dma((3,)),
        dma, dma, dma, dma, dma, dma,
        dma((3,)), dma((3,)),
        dma((2,)), dma((2, 4)),
        dma((2,)), dma((2, 4)), dma((2, 4)), dma((2, 4)),
        dma, dma((4,)), dma((4,)), dma((4,)),
        dma, dma((4,)),
        dma((2, 2)),
        dma, dma, dma, dma, dma, dma, dma, dma,
    ]
    tokens = jax.ShapeDtypeStruct((TOK, D), BF)
    return pl.pallas_call(
        kernel,
        out_shape=(
            tokens,
            tokens,
            tokens,
            jax.ShapeDtypeStruct((1, D, HID), F32),
            jax.ShapeDtypeStruct((1, D, HID), F32),
            jax.ShapeDtypeStruct((1, HID, D), F32),
        ),
        in_specs=[vm] * 6 + [hbm] * 3,
        out_specs=(vm, vm, vm, hbm, hbm, hbm),
        scratch_shapes=scratch,
        compiler_params=pltpu.CompilerParams(
            collective_id=0, has_side_effects=True, vmem_limit_bytes=61 * 2**20
        ),
    )(expert_ids, combine_gates, queries, keys, values, out_grad, gate_w, up_w, down_w)


def solution(mesh):
    flat = P(("tm", "expert"), None)
    cube = P(("tm", "expert"), None, None)
    return jax.shard_map(
        body,
        mesh=mesh,
        in_specs=(flat,) * 6 + (cube,) * 3,
        out_specs=(flat,) * 3 + (cube,) * 3,
        check_vma=False,
    )
```

time: 702 us -> 266 us (0.38); the launches traced: 693 us -> 266 us
  waiting for transfers between devices: 319 us -> 0 us
  Pallas kernels: 0 us -> 246 us
  blocking collectives: 151 us -> 0 us
  matrix products: 84.1 us -> 0 us
  local copies, waits for them, and re-layouts: 89.3 us -> 19 us
  other arithmetic: 28.2 us -> 0 us
  between operations: 14.6 us -> 0.65 us
    pallas_call x0 -> x1, Pallas kernels: none -> 246 us  [body(): pl.pallas_call(kernel, out_shape=(tokens, tokens, tokens, jax.ShapeDtypeS...]
    all_to_all x1 -> x0, blocking collectives: 151 us -> none  [side_by_side(): lax.all_to_all(both, axis, split_axis=split_dim, concat_axis=concat_dim,...]
    psum x2 -> x0, waiting for transfers between devices: 140 us -> none  [the longest x1 71.8 us: body(): lax.psum(inclusive_back.astype(jnp.bfloat16), 'expert').astype(jnp.float32)]
    all_to_all x1 -> x0, waiting for transfers between devices: 99.5 us -> none  [body(): lax.all_to_all(payload.astype(jnp.bfloat16), ('tm', 'expert'), split_axis...]
    dot_general x16 -> x0, matrix products: 84.1 us -> none  [the longest x1 11.8 us: body(): inclusive = jnp.einsum('c,chab->hab', picks, everyone, precision=highest)]
    all_gather x2 -> x0, waiting for transfers between devices: 79.5 us -> none  [the longest x1 53.7 us: body(): everyone = lax.all_gather(local[None], 'tm', axis=0, tiled=True)]
    another operation x3 -> x0, local copies, waits for them, and re-layouts: 21.4 us -> none  [the longest x1 10.7 us: body(): grad_rows = got_g.reshape(-1, width)]
    reshape x6 -> x0, local copies, waits for them, and re-layouts: 16.1 us -> none  [the longest x1 3.65 us: body(): jnp.repeat(grad_f, 2, axis=0) * combine_gates.reshape(-1, 1)]
  transfers between devices with their start and end apart: 5 -> 0, of which waited for: 5 -> 0; matrix products, arithmetic and copies ran while one was open for 7% -> 0% of each run, Pallas kernels for 0% -> 0%
where the time goes in v1:
time: 266 us
  Pallas kernels  246 us (92%)
  local copies, waits for them, and re-layouts  19 us (7%)
    pallas_call x1, Pallas kernels, body(): pl.pallas_call(kernel, out_shape=(tokens, tokens, tokens, jax.ShapeDtypeS...  246 us
    unnamed x12, local copies, waits for them, and re-layouts  19 us

profile of v1, /device:TPU:1, one launch (start us, length us, event | category | flops | bytes accessed | tf_op | source)
XLA Modules:
  0.0 265.5 jit_solution(5776458246166061247)
XLA Ops:
  0.6 1.4 copy.15.ids
  2.0 1.4 copy.16.gates
  3.5 245.9 %shard_map.136 = (bf16[128,2048]{1,0:T(8,128)(2,1)}, bf16[128,2048]{1,0:T(8,128)(2,1)}, bf16[128,2048]{1,0:T(8,128)(2,1)}, f32[1,2048,512]{2,1,0:T(8,128)}, f32[...) custom-call(s32[128,2]{1,0:T(8,128)} %copy.15.ids, f32[128,2]{1,0:T(8,128)} %copy.16.gates, bf16[128,2048]{1,0:T(8,128)(2,1)} %q.1, ...), custom_call_target="tpu_custom_call" | custom-call | tf_op jit(solution)/shard_map/pallas_call | solution.py:518
  249.4 1.9 copy.23
  251.2 1.9 copy.24
  253.1 1.9 copy.25
  255.0 0.0 copy-start.1
  255.0 4.8 %copy.26 = f32[1,2048,512]{2,1,0:T(8,128)} copy(f32[1,2048,512]{2,1,0:T(8,128)} %get-tuple-element.15) | data formatting | bytes 8388608
  259.8 0.0 copy-done.1
  259.8 0.0 copy-start
  259.8 2.1 copy.27
  262.0 1.6 copy-done
  263.5 2.0 copy.28
Async XLA Ops:
  255.0 4.8 %copy-start.1 = (f32[1,2048,512]{2,1,0:T(8,128)S(1)}, f32[1,2048,512]{2,1,0:T(8,128)}, u32[]{:S(2)}) copy-start(f32[1,2048,512]{2,1,0:T(8,128)} %get-tuple-element.16) | copy-start | bytes 12582916
  259.8 3.7 %copy-start = (f32[1,512,2048]{2,1,0:T(8,128)S(1)}, f32[1,512,2048]{2,1,0:T(8,128)}, u32[]{:S(2)}) copy-start(f32[1,512,2048]{2,1,0:T(8,128)} %get-tuple-element.17) | copy-start | bytes 12582916

commit v2 on v1

--- a/solution.py
+++ b/solution.py
@@ -16,10 +16,12 @@
 NE = 32
 ROWS = NE * G
 CH = 8 * G
+HF = CH // 2
 BC = 512
 D = 2048
 HID = 512
 DY = (0, 1, 3, 2)
+STEPS = 4
 BF = jnp.bfloat16
 F32 = jnp.float32
 
@@ -51,12 +53,12 @@
 
 
 def kernel(
-    ids, gates, q, k, v, og, wg_h, wu_h, wd_h,
-    qg_o, kg_o, vg_o, dwg_o, dwu_o, dwd_o,
-    wg, wu, wd, sterm, srecv, sspan, stb, rtm, rt, xq, xg, pm, gs, sg, sh, yb, xb, mx, hid,
+    ids, gates, q, k_h, v_h, og, wg_h, wu_h, wd_h,
+    qg_o, ball_o, dwg_o, dwu_o, dwd_o,
+    k, v, wg, wu, wd, sterm, srecv, sspan, stb, rtm, rt, xq, xg, pm, gs, sg, sh, yb, xb, mx, hid,
     act, gg, ug, part, rin, rout, rcin, rsin, red, rr, mg, stage,
     bterm, bz, bspan, bown, ball, qgs, qgb,
-    wsem, st_s, st_r, sp_s, sp_r, sb_s, sb_r, xt_s, xt_r,
+    kvsem, wsem, st_s, st_r, sp_s, sp_r, sb_s, sb_r, xt_s, xt_r,
     sl_s, sl_r, mc_s, mc_l, mc_r, mc_f, rd_s, ri_r, rc_r, rs_r, rt_s, rt_r, stsem,
     bz_s, bz_r, bp_s, bp_r, bb_s, bb_r, qg_s, qg_r,
 ):
@@ -92,30 +94,22 @@
 
     lax.fori_loop(4, 32, greet_plane, 0)
 
+    kv_copies = []
+    for i, (src, dst) in enumerate(((k_h, k), (v_h, v))):
+        cp = pltpu.make_async_copy(src, dst, kvsem.at[i])
+        cp.start()
+        kv_copies.append(cp)
     w_copies = []
     for i, (src, dst) in enumerate(((wg_h, wg), (wu_h, wu), (wd_h, wd))):
         cp = pltpu.make_async_copy(src.at[0], dst, wsem.at[i])
         cp.start()
         w_copies.append(cp)
 
-    for h in range(16):
-        sl = slice(h * HD, (h + 1) * HD)
-        sterm[h] = tn(k[:, sl], v[:, sl]).astype(BF)
-
-    eye = lax.broadcasted_iota(jnp.int32, (TOK, TOK), 0) == lax.broadcasted_iota(
-        jnp.int32, (TOK, TOK), 1
-    )
     upper = lax.broadcasted_iota(jnp.int32, (TOK, TOK), 0) < lax.broadcasted_iota(
         jnp.int32, (TOK, TOK), 1
     )
     upper = jnp.where(upper, 1.0, 0.0).astype(BF)
-    idf = ids[...].astype(F32)
-    gf = gates[...]
-
-    def as_row(a, kk):
-        return jnp.sum(jnp.where(eye, a[:, kk : kk + 1], 0.0), axis=0, keepdims=True)
-
-    id_rows = [as_row(idf, kk) for kk in range(2)]
+    id_rows = [ids[kk : kk + 1, :].astype(F32) for kk in range(2)]
     lanes_e = lax.broadcasted_iota(jnp.int32, (NE, TOK), 0).astype(F32)
     hot = [jnp.where(lanes_e == r, 1.0, 0.0) for r in id_rows]
     earlier = nn((hot[0] + hot[1]).astype(BF), upper)
@@ -123,18 +117,11 @@
     for kk in range(2):
         pos = jnp.sum(hot[kk] * earlier, axis=0, keepdims=True)
         rtm[kk : kk + 1, :] = jnp.where(pos < CAP, id_rows[kk] * G + pos, -4096.0)
-        rtm[2 + kk : 3 + kk, :] = as_row(gf, kk)
+        rtm[2 + kk : 3 + kk, :] = gates[kk : kk + 1, :]
 
     pl.semaphore_wait(bar, 43)
 
-    def send_term(i, _):
-        eo = mod(e + i, 16)
-        ho = mod(eo, 4) * 4 + lax.div(eo, jnp.int32(4))
-        remote(sterm.at[ho], srecv.at[e], st_s, st_r, (tm, eo))
-        return 0
-
-    lax.fori_loop(1, 16, send_term, 0)
-    for i, (src, dst) in enumerate(((rtm, rt), (og, xg), (q, xq))):
+    def exchange(i, src, dst):
         for d in range(1, 4):
             xo = mod(x + d, 4)
             s = src if i == 0 else src.at[:, cols(xo)]
@@ -142,20 +129,22 @@
         s = src if i == 0 else src.at[:, cols(x)]
         pltpu.make_async_copy(s, dst.at[x], xt_r.at[i]).start()
 
-    drain(srecv.at[pl.ds(0, 15)], st_r)
-    srecv[e] = sterm[x * 4 + z]
-    sspan[tm] = jnp.sum(srecv[...].astype(F32), axis=0)
-
-    def send_span(i, _):
-        remote(sspan.at[tm], sspan.at[tm], sp_s, sp_r, (mod(tm + i, 8), e))
-        return 0
-
-    lax.fori_loop(1, 8, send_span, 0)
-
-    drain(rt, xt_r.at[0])
-
-    def build(b, _):
-        r0 = pl.multiple_of(b * 128, 128)
+    exchange(0, rtm, rt)
+    exchange(1, og, xg)
+
+    for cp in kv_copies:
+        cp.wait()
+    for h in range(16):
+        sl = slice(h * HD, (h + 1) * HD)
+        sterm[h] = tn(k[:, sl], v[:, sl]).astype(BF)
+
+    def send_term(i, _):
+        eo = mod(e + i, 16)
+        ho = mod(eo, 4) * 4 + lax.div(eo, jnp.int32(4))
+        remote(sterm.at[ho], srecv.at[e], st_s, st_r, (tm, eo))
+        return 0
+
+    def build(r0):
         ridx = (lax.broadcasted_iota(jnp.int32, (128, TOK), 0) + r0).astype(F32)
         acc = jnp.zeros((128, TOK), F32)
         for s in range(4):
@@ -165,9 +154,6 @@
             pm[pl.ds(r0, 128), s * TOK : (s + 1) * TOK] = jnp.where(m0 | m1, 1.0, 0.0).astype(BF)
             acc = acc + jnp.where(m0, a[2:3], 0.0) + jnp.where(m1, a[3:4], 0.0)
         gs[pl.ds(r0, 128), :] = jnp.broadcast_to(jnp.sum(acc, axis=1, keepdims=True), (128, TOK))
-        return 0
-
-    lax.fori_loop(0, ROWS // 128, build, 0)
 
     def plane_rows(yy):
         return pl.ds(pl.multiple_of(yy * CH, CH), CH)
@@ -206,40 +192,64 @@
         remote(ref, ref, mc_s.at[a], mc_l.at[a, j], right)
         remote(ref, ref, mc_s.at[a], mc_r.at[a, j], left)
 
+    def halves(j):
+        start = src_plane(j) * CH
+        return [pl.ds(pl.multiple_of(start + i * HF, HF), HF) for i in range(2)]
+
     def relay(a, j):
         rows = plane_rows(src_plane(j))
-        from_left = big[a].at[rows, cols(xl)]
-        from_right = big[a].at[rows, cols(xr)]
-        drain(from_left, mc_l.at[a, j])
-        if j % 2 == 0:
-            remote(from_left, from_left, mc_s.at[a], mc_f.at[a, j], right)
-        drain(from_right, mc_r.at[a, j])
-        if j % 2 == 1:
-            remote(from_right, from_right, mc_s.at[a], mc_f.at[a, j], left)
+        upper_half, lower_half = halves(j)
+        drain(big[a].at[rows, cols(xl)], mc_l.at[a, j])
+        ref = big[a].at[upper_half, cols(xl)]
+        remote(ref, ref, mc_s.at[a], mc_f.at[a, j], right)
+        drain(big[a].at[rows, cols(xr)], mc_r.at[a, j])
+        ref = big[a].at[lower_half, cols(xr)]
+        remote(ref, ref, mc_s.at[a], mc_f.at[a, j], left)
 
     def far(a, j):
         drain(big[a].at[plane_rows(src_plane(j)), cols(xf)], mc_f.at[a, j])
 
+    drain(rt, xt_r.at[0])
+
+    def build_all(b, _):
+        build(pl.multiple_of(b * 128, 128))
+        return 0
+
+    lax.fori_loop(0, ROWS // 128, build_all, 0)
     drain(xg, xt_r.at[1])
+    lax.fori_loop(1, 16, send_term, 0)
+    exchange(2, q, xq)
     for j in range(4):
         rows = plane_rows(dst_plane(j))
         got = nn(pm[rows, :], xg[...].reshape(4 * TOK, BC))
         sg[rows, :] = (got * gs[rows, 0:1]).astype(BF)
         to_plane(sg, yb, cols(x), sl_s.at[0], sl_r.at[0, j], dst_plane(j), j == 0)
 
+    for j in range(2):
+        wait_own(0, j)
+        cast(0, j)
+    drain(srecv.at[pl.ds(0, 15)], st_r)
+    srecv[e] = sterm[x * 4 + z]
+    sspan[tm] = jnp.sum(srecv[...].astype(F32), axis=0).astype(BF)
+
+    def send_span(i, _):
+        remote(sspan.at[tm], sspan.at[tm], sp_s, sp_r, (mod(tm + i, 8), e))
+        return 0
+
+    lax.fori_loop(1, 8, send_span, 0)
+    for j in range(2, 4):
+        wait_own(0, j)
+        cast(0, j)
+
     drain(sspan.at[pl.ds(0, 7)], sp_r)
     total = jnp.zeros((HD, HD), F32)
     for t in range(8):
-        total = total + jnp.where(t <= tm, sspan[t], 0.0)
+        total = total + jnp.where(t <= tm, sspan[t].astype(F32), 0.0)
     stb[z] = total.astype(BF)
     for d in range(1, 4):
         remote(stb.at[z], stb.at[z], sb_s, sb_r, (tm, mod(z + d, 4) * 4 + x))
-
-    wait_own(0, 0)
-    cast(0, 0)
-
+    drain(stb.at[pl.ds(0, 3)], sb_r)
     drain(xq, xt_r.at[2])
-    drain(stb.at[pl.ds(0, 3)], sb_r)
     for i in range(4):
         sl = slice(i * HD, (i + 1) * HD)
         m = nn(xq[:, :, sl].reshape(4 * TOK, HD), stb[i])
@@ -251,9 +261,6 @@
         sh[rows, :] = nn(pm[rows, :], hid[...]).astype(BF)
         to_plane(sh, xb, cols(x), sl_s.at[1], sl_r.at[1, j], dst_plane(j), j == 0)
 
-    for j in range(1, 4):
-        wait_own(0, j)
-        cast(0, j)
     for j in range(4):
         relay(0, j)
         wait_own(1, j)
@@ -289,19 +296,21 @@
             return 0
 
         lax.fori_loop(0, D // BC, part_cols, 0)
-        if j % 2 == 0:
-            remote(part.at[rows, cols(xf)], rin.at[j], rd_s, ri_r.at[j], right)
-            remote(part.at[rows, cols(xl)], rsin.at[j], rd_s, rs_r.at[j], left)
-        else:
-            remote(part.at[rows, cols(xf)], rin.at[j], rd_s, ri_r.at[j], left)
-            remote(part.at[rows, cols(xr)], rsin.at[j], rd_s, rs_r.at[j], right)
+        up_h, low_h = halves(j)
+        top, low = pl.ds(0, HF), pl.ds(HF, HF)
+        remote(part.at[up_h, cols(xf)], rin.at[j, top], rd_s, ri_r.at[j], right)
+        remote(part.at[low_h, cols(xf)], rin.at[j, low], rd_s, ri_r.at[j], left)
+        remote(part.at[up_h, cols(xl)], rsin.at[j, top], rd_s, rs_r.at[j], left)
+        remote(part.at[low_h, cols(xr)], rsin.at[j, low], rd_s, rs_r.at[j], right)
 
     def add_on(j):
-        rows = plane_rows(src_plane(j))
+        up_h, low_h = halves(j)
         drain(rin.at[j], ri_r.at[j])
-        near = xr if j % 2 == 0 else xl
-        rout[j] = (rin[j].astype(F32) + part[rows, cols(near)].astype(F32)).astype(BF)
-        remote(rout.at[j], rcin.at[j], rd_s, rc_r.at[j], right if j % 2 == 0 else left)
+        for h, rows, near, dev in ((0, up_h, xr, right), (1, low_h, xl, left)):
+            sl = slice(h * HF, (h + 1) * HF)
+            rout[j, sl] = (rin[j, sl].astype(F32) + part[rows, cols(near)].astype(F32)).astype(BF)
+            half = pl.ds(h * HF, HF)
+            remote(rout.at[j, half], rcin.at[j, half], rd_s, rc_r.at[j], dev)
 
     def finish(j):
         yy = src_plane(j)
@@ -362,31 +371,28 @@
 
     relay(1, 0)
     relay(1, 1)
+    relay(1, 2)
     compute(0)
-    relay(1, 2)
+    relay(1, 3)
     compute(1)
+    compute(2)
     add_on(0)
-    relay(1, 3)
-    compute(2)
+    compute(3)
     add_on(1)
-    compute(3)
     add_on(2)
+    add_on(3)
     finish(0)
+    finish(1)
     weights_in(0)
-    add_on(3)
-    finish(1)
     weights_in(1)
     finish(2)
     weights_in(2)
-    finish(3)
     weights_in(3)
     combine(0)
+    finish(3)
+    combine(1)
+    combine(2)
     weights_out(0)
-    combine(1)
-    weights_out(1)
-    combine(2)
-    weights_out(2)
-    weights_out(3)
     combine(3)
 
     for i in range(4):
@@ -405,6 +411,7 @@
     for d in range(1, 4):
         xo = mod(x + d, 4)
         remote(qgs.at[xo], qgb.at[x], qg_s, qg_r, (tm, z * 4 + xo))
+    weights_out(1)
     drain(bz.at[pl.ds(0, 3)], bz_r)
     bz[z] = bterm[z]
     bspan[tm] = jnp.sum(bz[...].astype(F32), axis=0).astype(BF)
@@ -414,6 +421,7 @@
         return 0
 
     lax.fori_loop(1, 8, send_back_span, 0)
+    weights_out(2)
     drain(bspan.at[pl.ds(0, 7)], bp_r)
     total = jnp.zeros((HD, HD), F32)
     for t in range(8):
@@ -425,6 +433,7 @@
         return 0
 
     lax.fori_loop(1, 16, send_back, 0)
+    weights_out(3)
     drain(qgb.at[pl.ds(0, 3)], qg_r)
     qgb[x] = qgs[x]
     for b in range(4):
@@ -432,10 +441,7 @@
     drain(ball.at[pl.ds(0, 15)], bb_r)
     ball[e] = bown[...]
     for eo in range(16):
-        h = (eo % 4) * 4 + eo // 4
-        sl = slice(h * HD, (h + 1) * HD)
-        kg_o[:, sl] = nt(v[:, sl], ball[eo]).astype(BF)
-        vg_o[:, sl] = nn(k[:, sl], ball[eo]).astype(BF)
+        ball_o[(eo % 4) * 4 + eo // 4] = ball[eo]
 
     drain(sterm.at[pl.ds(0, 15)], st_s)
     drain(sspan.at[pl.ds(0, 7)], sp_s)
@@ -461,17 +467,30 @@
         ).wait()
 
 
+def finish_kernel(qg, ball, k, v, dwg, dwu, dwd, qg_o, kg_o, vg_o, dwg_o, dwu_o, dwd_o):
+    qg_o[...] = qg[...]
+    dwg_o[...] = dwg[...]
+    dwu_o[...] = dwu[...]
+    dwd_o[...] = dwd[...]
+    for i in range(16 // STEPS):
+        sl = slice(i * HD, (i + 1) * HD)
+        kg_o[:, sl] = nt(v[:, sl], ball[i]).astype(BF)
+        vg_o[:, sl] = nn(k[:, sl], ball[i]).astype(BF)
+
+
 def body(queries, keys, values, out_grad, expert_ids, combine_gates, gate_w, up_w, down_w):
     vm = pl.BlockSpec(memory_space=pltpu.VMEM)
     hbm = pl.BlockSpec(memory_space=pl.ANY)
     dma = pltpu.SemaphoreType.DMA
     scratch = [
+        pltpu.VMEM((TOK, D), BF),
+        pltpu.VMEM((TOK, D), BF),
         pltpu.VMEM((D, HID), BF),
         pltpu.VMEM((D, HID), BF),
         pltpu.VMEM((HID, D), BF),
         pltpu.VMEM((16, HD, HD), BF),
         pltpu.VMEM((16, HD, HD), BF),
-        pltpu.VMEM((8, HD, HD), F32),
+        pltpu.VMEM((8, HD, HD), BF),
         pltpu.VMEM((4, HD, HD), BF),
         pltpu.VMEM((8, TOK), F32),
         pltpu.VMEM((4, 8, TOK), F32),
@@ -504,6 +523,7 @@
         pltpu.VMEM((16, HD, HD), BF),
         pltpu.VMEM((4, TOK, BC), BF),
         pltpu.VMEM((4, TOK, BC), BF),
+        dma((2,)),
         dma((3,)),
         dma, dma, dma, dma, dma, dma,
         dma((3,)), dma((3,)),
@@ -515,23 +535,34 @@
         dma, dma, dma, dma, dma, dma, dma, dma,
     ]
     tokens = jax.ShapeDtypeStruct((TOK, D), BF)
-    return pl.pallas_call(
+    grads_in = jax.ShapeDtypeStruct((1, D, HID), F32)
+    grads_out = jax.ShapeDtypeStruct((1, HID, D), F32)
+    query_grad, back, gate_g, up_g, down_g = pl.pallas_call(
         kernel,
         out_shape=(
             tokens,
-            tokens,
-            tokens,
-            jax.ShapeDtypeStruct((1, D, HID), F32),
-            jax.ShapeDtypeStruct((1, D, HID), F32),
-            jax.ShapeDtypeStruct((1, HID, D), F32),
+            jax.ShapeDtypeStruct((16, HD, HD), BF),
+            grads_in,
+            grads_in,
+            grads_out,
         ),
-        in_specs=[vm] * 6 + [hbm] * 3,
-        out_specs=(vm, vm, vm, hbm, hbm, hbm),
+        in_specs=[vm] * 2 + [hbm] * 7,
+        out_specs=(vm, vm, hbm, hbm, hbm),
         scratch_shapes=scratch,
         compiler_params=pltpu.CompilerParams(
             collective_id=0, has_side_effects=True, vmem_limit_bytes=61 * 2**20
         ),
-    )(expert_ids, combine_gates, queries, keys, values, out_grad, gate_w, up_w, down_w)
+    )(expert_ids.T, combine_gates.T, queries, keys, values, out_grad, gate_w, up_w, down_w)
+    lanes = pl.BlockSpec((TOK, D // STEPS), lambda i: (0, i))
+    wide = pl.BlockSpec((1, D // STEPS, HID), lambda i: (0, i, 0))
+    tall = pl.BlockSpec((1, HID // STEPS, D), lambda i: (0, i, 0))
+    return pl.pallas_call(
+        finish_kernel,
+        out_shape=(tokens, tokens, tokens, grads_in, grads_in, grads_out),
+        grid=(STEPS,),
+        in_specs=[lanes, pl.BlockSpec((16 // STEPS, HD, HD), lambda i: (i, 0, 0)), lanes, lanes, wide, wide, tall],
+        out_specs=(lanes, lanes, lanes, wide, wide, tall),
+    )(query_grad, back, keys, values, gate_g, up_g, down_g)
 
 
 def solution(mesh):

time: 266 us -> 244 us (0.917)
  local copies, waits for them, and re-layouts: 19 us -> 0 us
    unnamed x12 -> x0, local copies, waits for them, and re-layouts: 19 us -> none
    pallas_call x1 -> x2, Pallas kernels: 246 us -> 244 us  [the longest x1 233 us: body(): pl.pallas_call(kernel, out_shape=(tokens, jax.ShapeDtypeStruct((16, HD, H...]
where the time goes in v2:
time: 244 us
  Pallas kernels  244 us (100%)
    pallas_call x1, Pallas kernels, body(): pl.pallas_call(kernel, out_shape=(tokens, jax.ShapeDtypeStruct((16, HD, H...  233 us
    pallas_call x1, Pallas kernels, body(): pl.pallas_call(finish_kernel, out_shape=(tokens, tokens, tokens, grads_in...  10.2 us

profile of v2, /device:TPU:1, one launch (start us, length us, event | category | flops | bytes accessed | tf_op | source)
XLA Modules:
  0.0 244.2 jit_solution(10195418762969131135)
XLA Ops:
  0.6 233.4 %shard_map.136 = (bf16[128,2048]{1,0:T(8,128)(2,1)}, bf16[16,128,128]{2,1,0:T(8,128)(2,1)}, f32[1,2048,512]{2,1,0:T(8,128)}, f32[1,2048,512]{2,1,0:T(8,128)}, f32[1,512,2048]{2,1,0:T(8,128)}) custom-call(s32[2,128]{1,0:T(2,128)} %bitcast.2, f32[2,128]{1,0:T(2,128)} %bitcast.3, bf16[128,2048]{1,0:T(8,128)(2,1)} %q.1, bf16[128,2048]{1,0:T(8,128)(2,1)} %k.1, ...), custom_call_target="tpu_custom_call" | custom-call | tf_op jit(solution)/shard_map/pallas_call | solution.py:540
  234.0 10.2 %shard_map.137 = (bf16[128,2048]{1,0:T(8,128)(2,1)}, bf16[128,2048]{1,0:T(8,128)(2,1)}, bf16[128,2048]{1,0:T(8,128)(2,1)}, f32[1,2048,512]{2,1,0:T(8,128)}, f32[...) custom-call(bf16[128,2048]{1,0:T(8,128)(2,1)} %get-tuple-element.11.qg, bf16[16,128,128]{2,1,0:T(8,128)(2,1)} %get-tuple-element.12.ball, ...), custom_call_target="tpu_custom_call" | custom-call | tf_op jit(solution)/shard_map/pallas_call | solution.py:559

commit v3 on v2

--- a/solution.py
+++ b/solution.py
@@ -55,10 +55,10 @@
 def kernel(
     ids, gates, q, k_h, v_h, og, wg_h, wu_h, wd_h,
     qg_o, ball_o, dwg_o, dwu_o, dwd_o,
-    k, v, wg, wu, wd, sterm, srecv, sspan, stb, rtm, rt, xq, xg, pm, gs, sg, sh, yb, xb, mx, hid,
+    k, v, wg, wu, wd, sterm, srecv, szsum, sxrecv, sspan, stb, rtm, rt, xq, xg, pm, gs, sg, sh, yb, xb, mx, hid,
     act, gg, ug, part, rin, rout, rcin, rsin, red, rr, mg, stage,
     bterm, bz, bspan, bown, ball, qgs, qgb,
-    kvsem, wsem, st_s, st_r, sp_s, sp_r, sb_s, sb_r, xt_s, xt_r,
+    kvsem, wsem, st_s, st_r, sx_s, sx_r, sp_s, sp_r, sb_s, sb_r, xt_s, xt_r,
     sl_s, sl_r, mc_s, mc_l, mc_r, mc_f, rd_s, ri_r, rc_r, rs_r, rt_s, rt_r, stsem,
     bz_s, bz_r, bp_s, bp_r, bb_s, bb_r, qg_s, qg_r,
 ):
@@ -136,13 +136,11 @@
         cp.wait()
     for h in range(16):
         sl = slice(h * HD, (h + 1) * HD)
-        sterm[h] = tn(k[:, sl], v[:, sl]).astype(BF)
-
-    def send_term(i, _):
-        eo = mod(e + i, 16)
-        ho = mod(eo, 4) * 4 + lax.div(eo, jnp.int32(4))
-        remote(sterm.at[ho], srecv.at[e], st_s, st_r, (tm, eo))
-        return 0
+        sterm[h % 4, h // 4] = tn(k[:, sl], v[:, sl]).astype(BF)
+
+    for d in range(1, 4):
+        zo = mod(z + d, 4)
+        remote(sterm.at[zo], srecv.at[z], st_s, st_r, (tm, zo * 4 + x))
 
     def build(r0):
         ridx = (lax.broadcasted_iota(jnp.int32, (128, TOK), 0) + r0).astype(F32)
@@ -217,7 +215,12 @@
 
     lax.fori_loop(0, ROWS // 128, build_all, 0)
     drain(xg, xt_r.at[1])
-    lax.fori_loop(1, 16, send_term, 0)
+    drain(srecv.at[pl.ds(0, 3)], st_r)
+    srecv[z] = sterm[z]
+    szsum[...] = jnp.sum(srecv[...].astype(F32), axis=0).astype(BF)
+    for d in range(1, 4):
+        xo = mod(x + d, 4)
+        remote(szsum.at[xo], sxrecv.at[x], sx_s, sx_r, (tm, z * 4 + xo))
     exchange(2, q, xq)
     for j in range(4):
         rows = plane_rows(dst_plane(j))
@@ -228,9 +231,9 @@
     for j in range(2):
         wait_own(0, j)
         cast(0, j)
-    drain(srecv.at[pl.ds(0, 15)], st_r)
-    srecv[e] = sterm[x * 4 + z]
-    sspan[tm] = jnp.sum(srecv[...].astype(F32), axis=0).astype(BF)
+    drain(sxrecv.at[pl.ds(0, 3)], sx_r)
+    sxrecv[x] = szsum[x]
+    sspan[tm] = jnp.sum(sxrecv[...].astype(F32), axis=0).astype(BF)
 
     def send_span(i, _):
         remote(sspan.at[tm], sspan.at[tm], sp_s, sp_r, (mod(tm + i, 8), e))
@@ -342,8 +345,8 @@
         def one(n, _):
             r = pl.ds(pl.multiple_of(n * 256, 256), 256)
             xt = xb[:, pl.ds(pl.multiple_of(s * 512 + n * 256, 256), 256)]
-            stage[slot, 0, r, :] = tn(xt, gg[...])
-            stage[slot, 1, r, :] = tn(xt, ug[...])
+            stage[slot, 0, r, :] = tn(xt, gg[...]).astype(BF)
+            stage[slot, 1, r, :] = tn(xt, ug[...]).astype(BF)
             return 0
 
         lax.fori_loop(0, 2, one, 0)
@@ -361,7 +364,7 @@
 
         def one(n, _):
             r = pl.ds(pl.multiple_of(n * 256, 256), 256)
-            stage[slot, w, r, :] = tn(act[:, r], yb[:, s * 512 : (s + 1) * 512])
+            stage[slot, w, r, :] = tn(act[:, r], yb[:, s * 512 : (s + 1) * 512]).astype(BF)
             return 0
 
         lax.fori_loop(0, 2, one, 0)
@@ -443,7 +446,8 @@
     for eo in range(16):
         ball_o[(eo % 4) * 4 + eo // 4] = ball[eo]
 
-    drain(sterm.at[pl.ds(0, 15)], st_s)
+    drain(srecv.at[pl.ds(0, 3)], st_s)
+    drain(sxrecv.at[pl.ds(0, 3)], sx_s)
     drain(sspan.at[pl.ds(0, 7)], sp_s)
     drain(stb.at[pl.ds(0, 3)], sb_s)
     drain(rt.at[pl.ds(0, 3)], xt_s.at[0])
@@ -469,9 +473,9 @@
 
 def finish_kernel(qg, ball, k, v, dwg, dwu, dwd, qg_o, kg_o, vg_o, dwg_o, dwu_o, dwd_o):
     qg_o[...] = qg[...]
-    dwg_o[...] = dwg[...]
-    dwu_o[...] = dwu[...]
-    dwd_o[...] = dwd[...]
+    dwg_o[...] = dwg[...].astype(F32)
+    dwu_o[...] = dwu[...].astype(F32)
+    dwd_o[...] = dwd[...].astype(F32)
     for i in range(16 // STEPS):
         sl = slice(i * HD, (i + 1) * HD)
         kg_o[:, sl] = nt(v[:, sl], ball[i]).astype(BF)
@@ -488,8 +492,10 @@
         pltpu.VMEM((D, HID), BF),
         pltpu.VMEM((D, HID), BF),
         pltpu.VMEM((HID, D), BF),
-        pltpu.VMEM((16, HD, HD), BF),
-        pltpu.VMEM((16, HD, HD), BF),
+        pltpu.VMEM((4, 4, HD, HD), BF),
+        pltpu.VMEM((4, 4, HD, HD), BF),
+        pltpu.VMEM((4, HD, HD), BF),
+        pltpu.VMEM((4, HD, HD), BF),
         pltpu.VMEM((8, HD, HD), BF),
         pltpu.VMEM((4, HD, HD), BF),
         pltpu.VMEM((8, TOK), F32),
@@ -515,7 +521,7 @@
         pltpu.VMEM((ROWS, BC), BF),
         pltpu.VMEM((ROWS, BC), BF),
         pltpu.VMEM((4 * TOK, BC), F32),
-        pltpu.VMEM((2, 2, 512, 512), F32),
+        pltpu.VMEM((2, 2, 512, 512), BF),
         pltpu.VMEM((4, HD, HD), BF),
         pltpu.VMEM((4, HD, HD), BF),
         pltpu.VMEM((8, HD, HD), BF),
@@ -525,7 +531,7 @@
         pltpu.VMEM((4, TOK, BC), BF),
         dma((2,)),
         dma((3,)),
-        dma, dma, dma, dma, dma, dma,
+        dma, dma, dma, dma, dma, dma, dma, dma,
         dma((3,)), dma((3,)),
         dma((2,)), dma((2, 4)),
         dma((2,)), dma((2, 4)), dma((2, 4)), dma((2, 4)),
@@ -542,9 +548,9 @@
         out_shape=(
             tokens,
             jax.ShapeDtypeStruct((16, HD, HD), BF),
-            grads_in,
-            grads_in,
-            grads_out,
+            jax.ShapeDtypeStruct((1, D, HID), BF),
+            jax.ShapeDtypeStruct((1, D, HID), BF),
+            jax.ShapeDtypeStruct((1, HID, D), BF),
         ),
         in_specs=[vm] * 2 + [hbm] * 7,
         out_specs=(vm, vm, hbm, hbm, hbm),

time: 244 us -> 236 us (0.967)
  Pallas kernels: 244 us -> 235 us
    pallas_call x1, Pallas kernels: 233 us -> 226 us  [body(): pl.pallas_call(kernel, out_shape=(tokens, jax.ShapeDtypeStruct((16, HD, H...]
where the time goes in v3:
time: 236 us
  Pallas kernels  235 us (100%)
    pallas_call x1, Pallas kernels, body(): pl.pallas_call(kernel, out_shape=(tokens, jax.ShapeDtypeStruct((16, HD, H...  226 us
    pallas_call x1, Pallas kernels, body(): pl.pallas_call(finish_kernel, out_shape=(tokens, tokens, tokens, grads_in...  8.93 us

profile of v3, /device:TPU:1, one launch (start us, length us, event | category | flops | bytes accessed | tf_op | source)
XLA Modules:
  0.0 236.0 jit_solution(12315305445734829188)
XLA Ops:
  0.6 226.4 %shard_map.136 = (bf16[128,2048]{1,0:T(8,128)(2,1)}, bf16[16,128,128]{2,1,0:T(8,128)(2,1)}, bf16[1,2048,512]{2,1,0:T(8,128)(2,1)}, bf16[1,2048,512]{2,1,0:T(8,128)(2,1)}, bf16[1,512,2048]{2,1,0:T(8,128)(2,1)}) custom-call(s32[2,128]{1,0:T(2,128)} %bitcast.2, f32[2,128]{1,0:T(2,128)} %bitcast.3, bf16[128,2048]{1,0:T(8,128)(2,1)} %q.1, bf16[128,2048]{1,0:T(8,128)(2,1)} %k.1, ...), custom_call_target="tpu_custom_call" | custom-call | tf_op jit(solution)/shard_map/pallas_call | solution.py:546
  227.0 8.9 %shard_map.137 = (bf16[128,2048]{1,0:T(8,128)(2,1)}, bf16[128,2048]{1,0:T(8,128)(2,1)}, bf16[128,2048]{1,0:T(8,128)(2,1)}, f32[1,2048,512]{2,1,0:T(8,128)}, f32[...) custom-call(bf16[128,2048]{1,0:T(8,128)(2,1)} %get-tuple-element.11.qg, bf16[16,128,128]{2,1,0:T(8,128)(2,1)} %get-tuple-element.12.ball, ...), custom_call_target="tpu_custom_call" | custom-call | tf_op jit(solution)/shard_map/pallas_call | solution.py:565
